TPU v7x, 32 devices: a whole 2x2x4 slice. The times are simulated.
32 devices in a mesh: state: 4 (over y, core), walker: 8 (over z, x).
Axes of the slice: x: 2, y: 2, z: 4, core: 2. Of those that a mesh axis runs over, the one named last changes fastest.
Arguments:
- walkers: float32 [8, 8, 126], P('state', 'walker'), may hold values from -8 to 8
- nuclei: float32 [12, 3], replicated, may hold values from -5 to 5
- w_embed: float32 [8, 48, 256], P('state'), may hold values from -0.875 to 0.875
- w_query: float32 [8, 1, 256, 256], P('state'), may hold values from -16 to 16
- w_key: float32 [8, 1, 256, 256], P('state'), may hold values from -0.375 to 0.375
- w_value: float32 [8, 1, 256, 256], P('state'), may hold values from -0.375 to 0.375
- w_attn_out: float32 [8, 1, 256, 256], P('state'), may hold values from -0.375 to 0.375
- w_mlp: float32 [8, 1, 256, 256], P('state'), may hold values from -0.375 to 0.375
- b_mlp: float32 [8, 1, 256], P('state'), may hold values from -3 to 3
- w_out: float32 [8, 256], P('state'), may hold values from -0.375 to 0.375
Outputs:
- margins: float32 [8, 8], replicated
- grad_embed: float32 [8, 48, 256], P('state')
- grad_query: float32 [8, 1, 256, 256], P('state')
- grad_key: float32 [8, 1, 256, 256], P('state')
- grad_value: float32 [8, 1, 256, 256], P('state')
- grad_attn_out: float32 [8, 1, 256, 256], P('state')
- grad_mlp: float32 [8, 1, 256, 256], P('state')
- grad_bias: float32 [8, 1, 256], P('state')
- grad_out: float32 [8, 256], P('state')
All inputs are finite; a program needn't handle non-finite values.
Results may differ from a plain program's by a relative error of at most 0.0003.
Values sent between devices are 32-bit elements; how exact they have to be, the bound alone decides.
A program may use at most 64 MiB of HBM per device.

v0:
```python
import functools
import math

import jax
import jax.numpy as jnp
from jax import lax
from jax.experimental import pallas as pl
from jax.experimental.pallas import tpu as pltpu
from jax.sharding import PartitionSpec as P

HEADS = 4
EPS = 1e-05
F32 = jnp.float32
BF16 = jnp.bfloat16
MESH = pl.DeviceIdType.MESH
WALKERS_PER_BLOCK = 4

NN = (((1,), (0,)), ((), ()))
NT = (((1,), (1,)), ((), ()))
TN = (((0,), (0,)), ((), ()))


def split(x, parts):
    out = []
    for part in range(parts):
        piece = x.astype(BF16)
        out.append(piece)
        if part + 1 < parts:
            x = x - piece.astype(F32)
    return out


def product(a, b, dims, parts):
    total = None
    for order in range(parts - 1, -1, -1):
        for i in range(order + 1):
            term = lax.dot_general(a[i], b[order - i], dims, preferred_element_type=F32)
            total = term if total is None else total + term
    return total


def normalise(hidden):
    centre = hidden - jnp.mean(hidden, axis=-1, keepdims=True)
    spread = jnp.mean(centre * centre, axis=-1, keepdims=True)
    scale = 1.0 / jnp.sqrt(spread + EPS)
    return centre * scale, scale


def normalise_back(grad, normed, scale):
    mean = jnp.mean(grad, axis=-1, keepdims=True)
    along = jnp.mean(grad * normed, axis=-1, keepdims=True)
    return scale * (grad - mean - normed * along)


def kernel(
    cfg,
    walkers, nuclei, w_embed, w_query, w_key, w_value, w_attn, w_mlp, b_mlp, w_out,
    margins, o_query, o_key, o_value, o_attn, o_mlp, o_extra,
    wbuf, raw_embed, raw, vecs, s_embed, s_w, feats, x1, r1, q, k, v, att, mixed, x2, r2, act, h2,
    g1, gk, gq, gv, dm, lrow, tab, part, part_extra, rbuf, rbuf_extra, ccol,
    load_sem, walk_send, walk_recv, tab_send, tab_recv, rs_send, rs_recv, ag_send, ag_recv,
):
    S, W, L, G, N, NE, PAD, D, FEAT, CH, EC = cfg
    held = N * L
    head_size = D // HEADS
    WB = WALKERS_PER_BLOCK
    RB = WB * PAD
    blocks = held // WB
    total_walkers = W
    s = lax.axis_index("state")
    w = lax.axis_index("walker")
    j = lax.div(w, G)
    g = lax.rem(w, G)
    net = s * L + j
    me = s * W + w

    loads = [pltpu.make_async_copy(w_embed.at[j], raw_embed, load_sem.at[0])]
    for n, ref in enumerate((w_query, w_key, w_value, w_attn, w_mlp)):
        loads.append(pltpu.make_async_copy(ref.at[j, 0], raw.at[n], load_sem.at[1 + n]))
    for copy in loads:
        copy.start()

    barrier = pltpu.get_barrier_semaphore()

    def greet(d, carry):
        other = lax.rem(me + d, S * W)
        pl.semaphore_signal(
            barrier, inc=1, device_id=(lax.div(other, W), lax.rem(other, W)), device_id_type=MESH
        )
        return carry

    lax.fori_loop(1, S * W, greet, 0)

    for copy in loads:
        copy.wait()
    for i, piece in enumerate(split(raw_embed[...], 3)):
        s_embed[i] = piece
    for n in range(5):
        for i, piece in enumerate(split(raw[n], 3 if n < 2 else 2)):
            s_w[n, i] = piece
    vecs[0:1, :] = b_mlp[j]
    vecs[1:2, :] = w_out[pl.ds(j, 1), :]

    pl.semaphore_wait(barrier, S * W - 1)

    def walk_copy(s_to, j_to):
        return pltpu.make_async_remote_copy(
            src_ref=walkers,
            dst_ref=wbuf.at[s, lax.rem(w, L)],
            send_sem=walk_send.at[s_to, j_to],
            recv_sem=walk_recv.at[s, lax.rem(w, L)],
            device_id=(s_to, j_to * G + lax.div(w, L)),
            device_id_type=MESH,
        )

    def walk_arrival(s_from, x_from):
        return pltpu.make_async_remote_copy(
            src_ref=walkers,
            dst_ref=wbuf.at[s_from, x_from],
            send_sem=walk_send.at[0, 0],
            recv_sem=walk_recv.at[s_from, x_from],
            device_id=(s_from, L * g + x_from),
            device_id_type=MESH,
        )

    for s_to in range(S):
        for j_to in range(L):
            to_me = s_to * W + j_to * G + lax.div(w, L) == me

            @pl.when(jnp.logical_not(to_me))
            def _():
                walk_copy(s_to, j_to).start()

            @pl.when(to_me)
            def _():
                wbuf[s, lax.rem(w, L)] = walkers[...]

    lane = lax.broadcasted_iota(jnp.int32, (1, 128), 1)
    atoms = nuclei.shape[0]
    owner = lax.broadcasted_iota(jnp.int32, (atoms, 128), 0) == lax.div(
        lax.broadcasted_iota(jnp.int32, (atoms, 128), 1), 4
    )
    nuc = [
        jnp.sum(jnp.where(owner, nuclei[:, c : c + 1], 0.0), axis=0, keepdims=True)
        for c in range(3)
    ]
    kind = lax.rem(lane, 4)
    row_of = lax.broadcasted_iota(jnp.int32, (PAD, 3 * NE), 0)
    col_of = lax.broadcasted_iota(jnp.int32, (PAD, 3 * NE), 1)
    pick = [col_of == row_of * 3 + c for c in range(3)]
    live = lax.broadcasted_iota(jnp.int32, (PAD, 1), 0) < NE

    for s_from in range(S):
        for x_from in range(L):
            from_me = s_from * W + L * g + x_from == me

            @pl.when(jnp.logical_not(from_me))
            def _():
                walk_arrival(s_from, x_from).wait_recv()

    for s_to in range(S):
        for j_to in range(L):
            to_me = s_to * W + j_to * G + lax.div(w, L) == me

            @pl.when(jnp.logical_not(to_me))
            def _():
                walk_copy(s_to, j_to).wait_send()

    for i in range(N):
        for x in range(L):
            row = wbuf[i // L, x, i % L]
            pos = [
                jnp.sum(jnp.where(pick[c], row, 0.0), axis=1, keepdims=True) for c in range(3)
            ]
            off = [pos[c] - nuc[c] for c in range(3)]
            dist = jnp.sqrt(off[0] * off[0] + off[1] * off[1] + off[2] * off[2] + 1.0)
            f = jnp.where(
                kind == 0, off[0], jnp.where(kind == 1, off[1], jnp.where(kind == 2, off[2], dist))
            )
            p = i * L + x
            feats[p * PAD : (p + 1) * PAD, :] = f[:, :FEAT]

    head_of = lax.div(lax.broadcasted_iota(jnp.int32, (1, D), 1), head_size)
    head_mask = [jnp.where(head_of == h, 1.0, 0.0).astype(F32) for h in range(HEADS)]
    key_live = lax.broadcasted_iota(jnp.int32, (1, PAD), 1) < NE

    def stack_heads(x):
        return jnp.concatenate([x * head_mask[h] for h in range(HEADS)], axis=0)

    def merge_heads(x):
        return sum(x[h * PAD : (h + 1) * PAD] * head_mask[h] for h in range(HEADS))

    lrow[...] = jnp.zeros_like(lrow)

    def weights(n, parts):
        return [s_w[n, i] for i in range(parts)]

    def forward(b, carry):
        rows = pl.ds(pl.multiple_of(b * RB, RB), RB)
        h0 = product(split(feats[rows, :], 3), [s_embed[i] for i in range(3)], NN, 3)
        normed, scale = normalise(h0)
        x1[rows, :] = normed
        r1[rows, :] = scale
        xs = split(normed, 3)
        queries = product(xs, weights(0, 3), NN, 3)
        keys = product(xs, weights(1, 3), NN, 3)
        values = product(xs[:2], weights(2, 2), NN, 2)
        q[rows, :] = queries
        k[rows, :] = keys
        v[rows, :] = values
        ks = split(keys, 3)
        vs = split(values, 2)
        outs = []
        for i in range(WB):
            here = slice(i * PAD, (i + 1) * PAD)
            qs = split(stack_heads(queries[here]), 3)
            scores = product(qs, [piece[here] for piece in ks], NT, 3) / math.sqrt(head_size)
            scores = jnp.where(key_live, scores, -1e30)
            e = jnp.exp(scores - jnp.max(scores, axis=-1, keepdims=True))
            a = e / jnp.sum(e, axis=-1, keepdims=True)
            att[b * WB + i] = a
            outs.append(
                merge_heads(product(split(a, 2), [piece[here] for piece in vs], NN, 2))
            )
        mix = jnp.concatenate(outs, axis=0)
        mixed[rows, :] = mix
        h1 = h0 + product(split(mix, 2), weights(3, 2), NN, 2)
        normed2, scale2 = normalise(h1)
        x2[rows, :] = normed2
        r2[rows, :] = scale2
        t = jnp.tanh(product(split(normed2, 2), weights(4, 2), NN, 2) + vecs[0:1, :])
        act[rows, :] = t
        last = h1 + t
        h2[rows, :] = last
        out = last * vecs[1:2, :]
        for i in range(WB):
            here = slice(i * PAD, (i + 1) * PAD)
            value = jnp.sum(jnp.where(live, out[here], 0.0)) / NE
            lrow[...] += jnp.where(lane == b * WB + i, value, 0.0)
        return carry

    lax.fori_loop(0, blocks, forward, 0)

    def tab_copy(d):
        other = lax.rem(me + d, S * W)
        return pltpu.make_async_remote_copy(
            src_ref=lrow,
            dst_ref=tab.at[net, g],
            send_sem=tab_send.at[d],
            recv_sem=tab_recv.at[d],
            device_id=(lax.div(other, W), lax.rem(other, W)),
            device_id_type=MESH,
        )

    tab[net, g] = lrow[...]

    def start_tab(d, carry):
        tab_copy(d).start()
        return carry

    lax.fori_loop(1, S * W, start_tab, 0)

    def backward_top(b, carry):
        rows = pl.ds(pl.multiple_of(b * RB, RB), RB)
        gh = vecs[1:2, :] * (1.0 / NE)
        t = act[rows, :]
        dinner = gh * (1.0 - t * t)
        dx2 = product(split(dinner, 2), weights(4, 2), NT, 2)
        act[rows, :] = dinner
        dh1 = gh + normalise_back(dx2, x2[rows, :], r2[rows, :])
        g1[rows, :] = dh1
        dm[rows, :] = product(split(dh1, 2), weights(3, 2), NT, 2)
        return carry

    lax.fori_loop(0, blocks, backward_top, 0)

    def wait_tab(d, carry):
        other = lax.rem(me - d + S * W, S * W)
        wo = lax.rem(other, W)
        from_net = lax.div(other, W) * L + lax.div(wo, G)
        pltpu.make_async_remote_copy(
            src_ref=lrow,
            dst_ref=tab.at[from_net, lax.rem(wo, G)],
            send_sem=tab_send.at[d],
            recv_sem=tab_recv.at[d],
            device_id=(lax.div(other, W), wo),
            device_id_type=MESH,
        ).wait_recv()
        tab_copy(d).wait_send()
        return carry

    lax.fori_loop(1, S * W, wait_tab, 0)

    sub8 = lax.broadcasted_iota(jnp.int32, (N, 128), 0)
    lane8 = lax.broadcasted_iota(jnp.int32, (N, 128), 1)
    state8 = lax.div(lane8, L)
    home8 = jnp.where(state8 == sub8, 1.0, 0.0).astype(F32)
    ident = jnp.where(lane8 == sub8, 1.0, 0.0).astype(F32)

    def ratio_of(logs):
        logs = logs.reshape(N, 128)
        home = jnp.sum(logs * home8, axis=0, keepdims=True)
        return jnp.where(lane8 < held, jnp.exp(logs - home), 0.0)

    summed = ratio_of(tab[:, 0])
    for other in range(1, G):
        summed = summed + ratio_of(tab[:, other])
    coupled = jnp.zeros((N, 128), F32)
    table = jnp.zeros((N, 128), F32)
    for i in range(N):
        col = jnp.sum(jnp.where(state8 == i, summed, 0.0), axis=1, keepdims=True) / total_walkers
        coupled = jnp.where(sub8 == i, jnp.sum(col * home8, axis=0, keepdims=True), coupled)
        table = jnp.where(sub8 == i, jnp.sum(col * ident, axis=0, keepdims=True), table)
    margins[...] = table[:, :N]
    coupled = coupled * (1.0 - home8)
    ratio = ratio_of(tab[:, g])
    terms = coupled * ratio
    denominator = jnp.sum(terms, axis=0, keepdims=True)
    cot = (terms - home8 * denominator) / total_walkers
    cot = jnp.sum(jnp.where(sub8 == net, cot, 0.0), axis=0, keepdims=True)
    rows_of = lax.broadcasted_iota(jnp.int32, (held * PAD, 128), 0)
    first = lax.broadcasted_iota(jnp.int32, (held * PAD, 128), 1) * PAD
    inside = jnp.logical_and(rows_of >= first, rows_of < first + NE)
    ccol[...] = jnp.sum(jnp.where(inside, cot, 0.0), axis=1, keepdims=True)

    outs = (o_mlp, o_attn, o_value, o_key, o_query, o_extra)

    def rs_copy(m, d):
        to = lax.rem(g + d, G)
        if m < 5:
            src = part.at[m, pl.ds(pl.multiple_of(to * CH, CH), CH)]
            dst = rbuf.at[m, d - 1]
        else:
            src = part_extra.at[pl.ds(pl.multiple_of(to * EC, EC), EC)]
            dst = rbuf_extra.at[d - 1]
        return pltpu.make_async_remote_copy(
            src_ref=src,
            dst_ref=dst,
            send_sem=rs_send.at[m, d - 1],
            recv_sem=rs_recv.at[m, d - 1],
            device_id=(s, j * G + to),
            device_id_type=MESH,
        )

    def rs_start(m):
        for d in range(1, G):
            rs_copy(m, d).start()

    def piece(m, who):
        jj = lax.div(who, G)
        gg = lax.rem(who, G)
        if m < 5:
            return outs[m].at[jj, 0, pl.ds(pl.multiple_of(gg * CH, CH), CH)]
        return outs[m].at[jj, pl.ds(pl.multiple_of(gg * EC, EC), EC)]

    def rs_finish(m):
        for d in range(1, G):
            rs_copy(m, d).wait_recv()
        if m < 5:
            total = part[m, pl.ds(pl.multiple_of(g * CH, CH), CH)]
            for d in range(1, G):
                total = total + rbuf[m, d - 1]
            outs[m][j, 0, pl.ds(pl.multiple_of(g * CH, CH), CH)] = total
        else:
            total = part_extra[pl.ds(pl.multiple_of(g * EC, EC), EC)]
            for d in range(1, G):
                total = total + rbuf_extra[d - 1]
            outs[m][j, pl.ds(pl.multiple_of(g * EC, EC), EC)] = total

    odd = lax.rem(w, 2)
    place = (1 - odd) * lax.div(w, 2) + odd * (W - lax.div(w + 1, 2))

    def at_place(p):
        p = lax.rem(p + 2 * W, W)
        high = lax.div(p, W // 2)
        return (1 - high) * 2 * p + high * (2 * (W - p) - 1)

    def hops(m, way):
        return W // 2 if (m + way) % 2 == 0 else W - 1 - W // 2

    def ag_copy(m, way, t):
        step = 1 - 2 * way
        block = piece(m, at_place(place - step * t))
        return pltpu.make_async_remote_copy(
            src_ref=block,
            dst_ref=block,
            send_sem=ag_send.at[m, way, t],
            recv_sem=ag_recv.at[m, way, t],
            device_id=(s, at_place(place + step)),
            device_id_type=MESH,
        )

    def ag_arrival(m, way, t):
        step = 1 - 2 * way
        block = piece(m, at_place(place - step * (t + 1)))
        return pltpu.make_async_remote_copy(
            src_ref=block,
            dst_ref=block,
            send_sem=ag_send.at[m, way, t],
            recv_sem=ag_recv.at[m, way, t],
            device_id=(s, at_place(place - step)),
            device_id_type=MESH,
        )

    def ag_step(m, t):
        for way in range(2):
            if 0 < t <= hops(m, way):
                ag_arrival(m, way, t - 1).wait_recv()
            if t < hops(m, way):
                ag_copy(m, way, t).start()

    def ag_finish(m):
        for way in range(2):
            for t in range(hops(m, way)):
                ag_copy(m, way, t).wait_send()

    c = ccol[...]

    def outer(x, y):
        return product(split(x, 2), split(y * c, 2), TN, 2)

    part[0] = outer(x2[...], act[...])
    rs_start(0)
    part[1] = outer(mixed[...], g1[...])
    rs_start(1)

    def backward_attention(b, carry):
        rows = pl.ds(pl.multiple_of(b * RB, RB), RB)
        dq_list, dk_list, dv_list = [], [], []
        for i in range(WB):
            here = pl.ds(pl.multiple_of(b * RB + i * PAD, PAD), PAD)
            a = att[b * WB + i]
            dms = split(stack_heads(jnp.where(live, dm[here, :], 0.0)), 2)
            as_ = split(a, 2)
            vs = split(v[here, :], 2)
            ks = split(k[here, :], 2)
            qs = split(stack_heads(q[here, :]), 2)
            da = product(dms, vs, NT, 2)
            dv_list.append(product(as_, dms, TN, 2))
            ds = a * (da - jnp.sum(a * da, axis=-1, keepdims=True)) / math.sqrt(head_size)
            dss = split(ds, 2)
            dq_list.append(merge_heads(product(dss, ks, NN, 2)))
            dk_list.append(product(dss, qs, TN, 2))
        dq = jnp.concatenate(dq_list, axis=0)
        dk = jnp.concatenate(dk_list, axis=0)
        dv = jnp.concatenate(dv_list, axis=0)
        gq[rows, :] = dq
        gk[rows, :] = dk
        gv[rows, :] = dv
        dx1 = (
            product(split(dq, 2), weights(0, 2), NT, 2)
            + product(split(dk, 2), weights(1, 2), NT, 2)
            + product(split(dv, 2), weights(2, 2), NT, 2)
        )
        dm[rows, :] = g1[rows, :] + normalise_back(dx1, x1[rows, :], r1[rows, :])
        return carry

    lax.fori_loop(0, blocks, backward_attention, 0)

    part[2] = outer(x1[...], gv[...])
    rs_start(2)
    part[3] = outer(x1[...], gk[...])
    rs_start(3)
    part[4] = outer(x1[...], gq[...])
    rs_start(4)
    part_extra[...] = jnp.zeros_like(part_extra)
    part_extra[0:FEAT, :] = outer(feats[...], dm[...])
    part_extra[FEAT : FEAT + 1, :] = jnp.sum(act[...] * c, axis=0, keepdims=True)
    part_extra[FEAT + 1 : FEAT + 2, :] = jnp.sum(h2[...] * c, axis=0, keepdims=True) / NE
    rs_start(5)

    for m in range(6):
        rs_finish(m)
        ag_step(m, 0)
    for t in range(1, W // 2 + 1):
        for m in range(6):
            ag_step(m, t)
    for m in range(6):
        ag_finish(m)
        for d in range(1, G):
            rs_copy(m, d).wait_send()


def shards(walkers, nuclei, w_embed, w_query, w_key, w_value, w_attn_out, w_mlp, b_mlp, w_out):
    S = lax.axis_size("state")
    W = lax.axis_size("walker")
    L, per_device, coords = walkers.shape
    assert per_device == 1 and W % (2 * L) == 0
    G = W // L
    N = S * L
    NE = coords // 3
    PAD = -(-NE // 16) * 16
    FEAT, D = w_embed.shape[1:]
    CH = D // G
    rows_extra = max(-(-(FEAT + 2) // (8 * G)) * 8 * G, 8 * G)
    EC = rows_extra // G
    held = N * L
    R = held * PAD
    cfg = (S, W, L, G, N, NE, PAD, D, FEAT, CH, EC)
    vmem = pl.BlockSpec(memory_space=pltpu.VMEM)
    hbm = pl.BlockSpec(memory_space=pl.ANY)
    full = lambda: pltpu.VMEM((R, D), F32)
    column = lambda: pltpu.VMEM((R, 1), F32)
    weight = jax.ShapeDtypeStruct((L, 1, D, D), F32)
    dma = pltpu.SemaphoreType.DMA
    outs = pl.pallas_call(
        functools.partial(kernel, cfg),
        out_shape=(
            jax.ShapeDtypeStruct((N, N), F32),
            weight, weight, weight, weight, weight,
            jax.ShapeDtypeStruct((L, rows_extra, D), F32),
        ),
        in_specs=[vmem, vmem, hbm, hbm, hbm, hbm, hbm, hbm, vmem, vmem],
        out_specs=(vmem,) * 7,
        scratch_shapes=[
            pltpu.VMEM((S, L, L, 1, coords), F32),
            pltpu.VMEM((FEAT, D), F32),
            pltpu.VMEM((5, D, D), F32),
            pltpu.VMEM((8, D), F32),
            pltpu.VMEM((3, FEAT, D), BF16),
            pltpu.VMEM((5, 3, D, D), BF16),
            pltpu.VMEM((R, FEAT), F32),
            full(), column(), full(), full(), full(),
            pltpu.VMEM((held, HEADS * PAD, PAD), F32),
            full(), full(), column(), full(), full(),
            full(), full(), full(), full(), full(),
            pltpu.VMEM((1, 128), F32),
            pltpu.VMEM((N, G, 1, 128), F32),
            pltpu.VMEM((5, D, D), F32),
            pltpu.VMEM((rows_extra, D), F32),
            pltpu.VMEM((5, G - 1, CH, D), F32),
            pltpu.VMEM((G - 1, EC, D), F32),
            column(),
            dma((6,)),
            dma((S, L)), dma((S, L)),
            dma((S * W,)), dma((S * W,)),
            dma((6, G - 1)), dma((6, G - 1)),
            dma((6, 2, W // 2)), dma((6, 2, W // 2)),
        ],
        compiler_params=pltpu.CompilerParams(
            collective_id=0, has_side_effects=True, vmem_limit_bytes=56 * 1024 * 1024
        ),
    )(walkers, nuclei, w_embed, w_query, w_key, w_value, w_attn_out, w_mlp, b_mlp, w_out)
    margins, g_query, g_key, g_value, g_attn, g_mlp, extra = outs
    return (
        margins,
        extra[:, :FEAT],
        g_query, g_key, g_value, g_attn, g_mlp,
        extra[:, FEAT : FEAT + 1],
        extra[:, FEAT + 1],
    )


def solution(mesh):
    return jax.shard_map(
        shards,
        mesh=mesh,
        in_specs=(
            P("state", "walker", None),
            P(),
            P("state", None, None),
            P("state", None, None, None),
            P("state", None, None, None),
            P("state", None, None, None),
            P("state", None, None, None),
            P("state", None, None, None),
            P("state", None, None),
            P("state", None),
        ),
        out_specs=(
            P(),
            P("state", None, None),
            P("state", None, None, None),
            P("state", None, None, None),
            P("state", None, None, None),
            P("state", None, None, None),
            P("state", None, None, None),
            P("state", None, None),
            P("state", None),
        ),
        check_vma=False,
    )
```

profile of v0, /device:TPU:0, one launch (start us, length us, event | category | flops | bytes accessed | tf_op | source)
XLA Modules:
  0.0 101.1 jit_solution(6940257243771912752)
XLA Ops:
  0.6 1.4 %copy.19.nuclei = f32[12,3]{1,0:T(8,128)} copy(f32[12,3]{0,1:T(4,128)} %param.11) | data formatting | bytes 288 | tf_op args[1]
  2.0 88.5 %shard_map.169 = (f32[8,8]{1,0:T(8,128)}, f32[2,1,256,256]{3,2,1,0:T(8,128)}, f32[2,1,256,256]{3,2,1,0:T(8,128)}, f32[2,1,256,256]{3,2,1,0:T(8,128)}, f32[2,1,25...) custom-call(f32[2,1,126]{2,1,0:T(1,128)} %walkers.1, f32[12,3]{1,0:T(8,128)} %copy.19.nuclei, ...), custom_call_target="tpu_custom_call" | custom-call | tf_op jit(solution)/shard_map/pallas_call | solution.py:506
  90.5 1.4 %fusion = (f32[2,1,256]{2,1,0:T(1,128)S(1)}, f32[2,1,256]{2,1,0:T(1,128)}) fusion(f32[2,64,256]{2,1,0:T(8,128)} %get-tuple-element.17), kind=kLoop, calls=%fused_computation.1 | loop fusion | bytes 8192 | tf_op jit(solution)/shard_map/slice | solution.py:550
  91.9 1.5 %slice.9 = f32[2,48,256]{2,1,0:T(8,128)} slice(f32[2,64,256]{2,1,0:T(8,128)} %get-tuple-element.17), slice={[0:2], [0:48], [0:256]} | slice | bytes 196608 | tf_op jit(solution)/shard_map/slice | solution.py:547
  93.4 0.0 copy-start.4
  93.4 0.6 copy.22
  94.0 0.1 copy-done.4
  94.1 0.6 copy.29
  94.7 0.0 copy-start.3
  94.7 1.9 %copy.30 = f32[2,1,256,256]{3,2,1,0:T(8,128)} copy(f32[2,1,256,256]{3,2,1,0:T(8,128)} %get-tuple-element.36) | data formatting | bytes 1048576
  96.6 0.0 copy-done.3
  96.6 0.0 copy-start.2
  96.6 0.8 copy.31
  97.4 0.4 copy-done.2
  97.9 0.0 copy-start.1
  97.9 0.8 copy.32
  98.6 0.4 copy-done.1
  99.1 0.0 copy-start
  99.1 0.8 copy.33
  99.9 0.4 copy-done
  100.3 0.8 copy.34
Async XLA Ops:
  93.4 0.7 copy-start.4
  94.7 1.9 %copy-start.3 = (f32[2,1,256,256]{3,2,1,0:T(8,128)S(1)}, f32[2,1,256,256]{3,2,1,0:T(8,128)}, u32[]{:S(2)}) copy-start(f32[2,1,256,256]{3,2,1,0:T(8,128)} %get-tuple-element.37) | copy-start | bytes 1572868
  96.6 1.2 %copy-start.2 = (f32[2,1,256,256]{3,2,1,0:T(8,128)S(1)}, f32[2,1,256,256]{3,2,1,0:T(8,128)}, u32[]{:S(2)}) copy-start(f32[2,1,256,256]{3,2,1,0:T(8,128)} %get-tuple-element.38) | copy-start | bytes 1572868
  97.9 1.2 %copy-start.1 = (f32[2,1,256,256]{3,2,1,0:T(8,128)S(1)}, f32[2,1,256,256]{3,2,1,0:T(8,128)}, u32[]{:S(2)}) copy-start(f32[2,1,256,256]{3,2,1,0:T(8,128)} %get-tuple-element.39) | copy-start | bytes 1572868
  99.1 1.2 %copy-start = (f32[2,1,256,256]{3,2,1,0:T(8,128)S(1)}, f32[2,1,256,256]{3,2,1,0:T(8,128)}, u32[]{:S(2)}) copy-start(f32[2,1,256,256]{3,2,1,0:T(8,128)} %get-tuple-element.40) | copy-start | bytes 1572868
where the time goes:
time: 102 us; the launch traced here: 101 us
  Pallas kernels  88.5 us (87%)
  local copies, waits for them, and re-layouts  12 us (12%)
    pallas_call x1, Pallas kernels, shards(): pl.pallas_call(functools.partial(kernel, cfg), out_shape=(jax.ShapeDtypeS...  88.5 us
    unnamed x18, local copies, waits for them, and re-layouts  9.05 us

commit v1 on v0

--- a/solution.py
+++ b/solution.py
@@ -39,6 +39,23 @@
     return total
 
 
+def product_packed(a, b):
+    parts, width = len(a), b[0].shape[0]
+    stack = jnp.concatenate(b, axis=0)
+    sums = [None] * parts
+    for i in range(parts - 1, -1, -1):
+        wide = lax.dot_general(
+            a[i], stack[: (parts - i) * width], NT, preferred_element_type=F32
+        )
+        for n in range(parts - i):
+            term = wide[:, n * width : (n + 1) * width]
+            sums[i + n] = term if sums[i + n] is None else sums[i + n] + term
+    total = sums[-1]
+    for term in sums[-2::-1]:
+        total = total + term
+    return total
+
+
 def normalise(hidden):
     centre = hidden - jnp.mean(hidden, axis=-1, keepdims=True)
     spread = jnp.mean(centre * centre, axis=-1, keepdims=True)
@@ -54,11 +71,11 @@
 
 def kernel(
     cfg,
-    walkers, nuclei, w_embed, w_query, w_key, w_value, w_attn, w_mlp, b_mlp, w_out,
-    margins, o_query, o_key, o_value, o_attn, o_mlp, o_extra,
-    wbuf, raw_embed, raw, vecs, s_embed, s_w, feats, x1, r1, q, k, v, att, mixed, x2, r2, act, h2,
+    walkers, nuclei_in, w_embed, w_query, w_key, w_value, w_attn, w_mlp, b_mlp_in, w_out_in,
+    margins, f_mlp, f_attn, f_value, f_key, f_query, f_extra,
+    o_weights, o_extra, nuclei, b_mlp, w_out, wbuf, raw_embed, raw, vecs, s_embed, s_w, feats, x1, r1, q, k, v, att, mixed, x2, r2, act, h2,
     g1, gk, gq, gv, dm, lrow, tab, part, part_extra, rbuf, rbuf_extra, ccol,
-    load_sem, walk_send, walk_recv, tab_send, tab_recv, rs_send, rs_recv, ag_send, ag_recv,
+    load_sem, flush_sem, walk_send, walk_recv, tab_send, tab_recv, rs_send, rs_recv, ag_send, ag_recv,
 ):
     S, W, L, G, N, NE, PAD, D, FEAT, CH, EC = cfg
     held = N * L
@@ -77,6 +94,8 @@
     loads = [pltpu.make_async_copy(w_embed.at[j], raw_embed, load_sem.at[0])]
     for n, ref in enumerate((w_query, w_key, w_value, w_attn, w_mlp)):
         loads.append(pltpu.make_async_copy(ref.at[j, 0], raw.at[n], load_sem.at[1 + n]))
+    for n, (src, dst) in enumerate(((nuclei_in, nuclei), (b_mlp_in, b_mlp), (w_out_in, w_out))):
+        loads.append(pltpu.make_async_copy(src, dst, load_sem.at[6 + n]))
     for copy in loads:
         copy.start()
 
@@ -133,17 +152,18 @@
 
             @pl.when(to_me)
             def _():
-                wbuf[s, lax.rem(w, L)] = walkers[...]
+                own = pltpu.make_async_copy(walkers, wbuf.at[s, lax.rem(w, L)], load_sem.at[9])
+                own.start()
+                own.wait()
 
     lane = lax.broadcasted_iota(jnp.int32, (1, 128), 1)
-    atoms = nuclei.shape[0]
-    owner = lax.broadcasted_iota(jnp.int32, (atoms, 128), 0) == lax.div(
-        lax.broadcasted_iota(jnp.int32, (atoms, 128), 1), 4
-    )
-    nuc = [
-        jnp.sum(jnp.where(owner, nuclei[:, c : c + 1], 0.0), axis=0, keepdims=True)
-        for c in range(3)
-    ]
+    atom = lax.div(lane, 4)
+    nuc = []
+    for c in range(3):
+        along = jnp.zeros((1, 128), F32)
+        for a in range(nuclei.shape[1]):
+            along = jnp.where(atom == a, nuclei[c : c + 1, a : a + 1], along)
+        nuc.append(along)
     kind = lax.rem(lane, 4)
     row_of = lax.broadcasted_iota(jnp.int32, (PAD, 3 * NE), 0)
     col_of = lax.broadcasted_iota(jnp.int32, (PAD, 3 * NE), 1)
@@ -182,10 +202,11 @@
 
     head_of = lax.div(lax.broadcasted_iota(jnp.int32, (1, D), 1), head_size)
     head_mask = [jnp.where(head_of == h, 1.0, 0.0).astype(F32) for h in range(HEADS)]
+    head_mask_bf16 = [mask.astype(BF16) for mask in head_mask]
     key_live = lax.broadcasted_iota(jnp.int32, (1, PAD), 1) < NE
 
     def stack_heads(x):
-        return jnp.concatenate([x * head_mask[h] for h in range(HEADS)], axis=0)
+        return jnp.concatenate([x * head_mask_bf16[h] for h in range(HEADS)], axis=0)
 
     def merge_heads(x):
         return sum(x[h * PAD : (h + 1) * PAD] * head_mask[h] for h in range(HEADS))
@@ -208,13 +229,14 @@
         q[rows, :] = queries
         k[rows, :] = keys
         v[rows, :] = values
+        queries_split = split(queries, 3)
         ks = split(keys, 3)
         vs = split(values, 2)
         outs = []
         for i in range(WB):
             here = slice(i * PAD, (i + 1) * PAD)
-            qs = split(stack_heads(queries[here]), 3)
-            scores = product(qs, [piece[here] for piece in ks], NT, 3) / math.sqrt(head_size)
+            qs = [stack_heads(piece[here]) for piece in queries_split]
+            scores = product_packed(qs, [piece[here] for piece in ks]) / math.sqrt(head_size)
             scores = jnp.where(key_live, scores, -1e30)
             e = jnp.exp(scores - jnp.max(scores, axis=-1, keepdims=True))
             a = e / jnp.sum(e, axis=-1, keepdims=True)
@@ -323,7 +345,8 @@
     inside = jnp.logical_and(rows_of >= first, rows_of < first + NE)
     ccol[...] = jnp.sum(jnp.where(inside, cot, 0.0), axis=1, keepdims=True)
 
-    outs = (o_mlp, o_attn, o_value, o_key, o_query, o_extra)
+    outs = [o_weights.at[m] for m in range(5)] + [o_extra]
+    results = (f_mlp, f_attn, f_value, f_key, f_query, f_extra)
 
     def rs_copy(m, d):
         to = lax.rem(g + d, G)
@@ -408,11 +431,29 @@
                 ag_arrival(m, way, t - 1).wait_recv()
             if t < hops(m, way):
                 ag_copy(m, way, t).start()
+        if t == last:
+            flush(m).start()
+
+    last = W // 2
+
+    def flush(m):
+        return pltpu.make_async_copy(outs[m], results[m], flush_sem.at[m])
 
     def ag_finish(m):
         for way in range(2):
             for t in range(hops(m, way)):
                 ag_copy(m, way, t).wait_send()
+        flush(m).wait()
+
+    todo = [[("sum", 0)] + [("hop", t) for t in range(1, last + 1)] for m in range(6)]
+
+    def advance(*arrays):
+        for m in arrays:
+            if todo[m]:
+                what, t = todo[m].pop(0)
+                if what == "sum":
+                    rs_finish(m)
+                ag_step(m, t)
 
     c = ccol[...]
 
@@ -424,61 +465,94 @@
     part[1] = outer(mixed[...], g1[...])
     rs_start(1)
 
-    def backward_attention(b, carry):
-        rows = pl.ds(pl.multiple_of(b * RB, RB), RB)
-        dq_list, dk_list, dv_list = [], [], []
+    def stacked_gradient(here):
+        return [stack_heads(p) for p in split(jnp.where(live, dm[here, :], 0.0), 2)]
+
+    def backward_values(b, carry):
+        for i in range(WB):
+            here = pl.ds(pl.multiple_of(b * RB + i * PAD, PAD), PAD)
+            gv[here, :] = product(split(att[b * WB + i], 2), stacked_gradient(here), TN, 2)
+        return carry
+
+    lax.fori_loop(0, blocks, backward_values, 0)
+    part[2] = outer(x1[...], gv[...])
+    rs_start(2)
+    advance(0)
+    advance(1)
+
+    def backward_scores(b, carry):
         for i in range(WB):
             here = pl.ds(pl.multiple_of(b * RB + i * PAD, PAD), PAD)
             a = att[b * WB + i]
-            dms = split(stack_heads(jnp.where(live, dm[here, :], 0.0)), 2)
-            as_ = split(a, 2)
-            vs = split(v[here, :], 2)
             ks = split(k[here, :], 2)
-            qs = split(stack_heads(q[here, :]), 2)
-            da = product(dms, vs, NT, 2)
-            dv_list.append(product(as_, dms, TN, 2))
+            qs = [stack_heads(p) for p in split(q[here, :], 2)]
+            da = product_packed(stacked_gradient(here), split(v[here, :], 2))
             ds = a * (da - jnp.sum(a * da, axis=-1, keepdims=True)) / math.sqrt(head_size)
             dss = split(ds, 2)
-            dq_list.append(merge_heads(product(dss, ks, NN, 2)))
-            dk_list.append(product(dss, qs, TN, 2))
-        dq = jnp.concatenate(dq_list, axis=0)
-        dk = jnp.concatenate(dk_list, axis=0)
-        dv = jnp.concatenate(dv_list, axis=0)
-        gq[rows, :] = dq
-        gk[rows, :] = dk
-        gv[rows, :] = dv
-        dx1 = (
-            product(split(dq, 2), weights(0, 2), NT, 2)
-            + product(split(dk, 2), weights(1, 2), NT, 2)
-            + product(split(dv, 2), weights(2, 2), NT, 2)
-        )
-        dm[rows, :] = g1[rows, :] + normalise_back(dx1, x1[rows, :], r1[rows, :])
-        return carry
-
-    lax.fori_loop(0, blocks, backward_attention, 0)
-
-    part[2] = outer(x1[...], gv[...])
-    rs_start(2)
+            gq[here, :] = merge_heads(product(dss, ks, NN, 2))
+            gk[here, :] = product(dss, qs, TN, 2)
+
+        for bb in range(blocks):
+            arrays = ((0, 2), (0, 1), (0, 1, 2), (0, 1, 2))[bb % 4] if bb < 4 else ()
+
+            @pl.when(b == bb)
+            def _():
+                advance(*arrays)
+
+        return carry
+
+    lax.fori_loop(0, blocks, backward_scores, 0)
+
     part[3] = outer(x1[...], gk[...])
     rs_start(3)
     part[4] = outer(x1[...], gq[...])
     rs_start(4)
+    advance(1, 2)
+
+    def backward_embed(b, carry):
+        rows = pl.ds(pl.multiple_of(b * RB, RB), RB)
+        dx1 = (
+            product(split(gq[rows, :], 2), weights(0, 2), NT, 2)
+            + product(split(gk[rows, :], 2), weights(1, 2), NT, 2)
+            + product(split(gv[rows, :], 2), weights(2, 2), NT, 2)
+        )
+        dm[rows, :] = g1[rows, :] + normalise_back(dx1, x1[rows, :], r1[rows, :])
+        return carry
+
+    lax.fori_loop(0, blocks, backward_embed, 0)
+    advance(3, 4, 2)
     part_extra[...] = jnp.zeros_like(part_extra)
     part_extra[0:FEAT, :] = outer(feats[...], dm[...])
     part_extra[FEAT : FEAT + 1, :] = jnp.sum(act[...] * c, axis=0, keepdims=True)
     part_extra[FEAT + 1 : FEAT + 2, :] = jnp.sum(h2[...] * c, axis=0, keepdims=True) / NE
     rs_start(5)
-
-    for m in range(6):
-        rs_finish(m)
-        ag_step(m, 0)
-    for t in range(1, W // 2 + 1):
-        for m in range(6):
-            ag_step(m, t)
+    advance(3, 4)
+    while any(todo):
+        advance(*range(6))
     for m in range(6):
         ag_finish(m)
         for d in range(1, G):
             rs_copy(m, d).wait_send()
+
+
+def finish_kernel(
+    m_in, mlp, attn, value, key, query, extra,
+    margins, o_embed, o_query, o_key, o_value, o_attn, o_mlp, o_bias, o_out, sem,
+):
+    feat = o_embed.shape[1]
+    margins[...] = m_in[...]
+    copies = []
+    for src, dst in ((query, o_query), (key, o_key), (value, o_value), (attn, o_attn), (mlp, o_mlp)):
+        for n in range(dst.shape[0]):
+            copies.append(pltpu.make_async_copy(src.at[n], dst.at[n], sem.at[len(copies)]))
+    for copy in copies:
+        copy.start()
+    for n in range(o_embed.shape[0]):
+        o_embed[n] = extra[n, :feat]
+        o_bias[n] = extra[n, feat : feat + 1]
+        o_out[n : n + 1, :] = extra[n, feat + 1 : feat + 2]
+    for copy in copies:
+        copy.wait()
 
 
 def shards(walkers, nuclei, w_embed, w_query, w_key, w_value, w_attn_out, w_mlp, b_mlp, w_out):
@@ -510,9 +584,14 @@
             weight, weight, weight, weight, weight,
             jax.ShapeDtypeStruct((L, rows_extra, D), F32),
         ),
-        in_specs=[vmem, vmem, hbm, hbm, hbm, hbm, hbm, hbm, vmem, vmem],
-        out_specs=(vmem,) * 7,
+        in_specs=[hbm] * 10,
+        out_specs=(vmem,) + (hbm,) * 6,
         scratch_shapes=[
+            pltpu.VMEM((5, L, 1, D, D), F32),
+            pltpu.VMEM((L, rows_extra, D), F32),
+            pltpu.VMEM(nuclei.shape[::-1], F32),
+            pltpu.VMEM(b_mlp.shape, F32),
+            pltpu.VMEM(w_out.shape, F32),
             pltpu.VMEM((S, L, L, 1, coords), F32),
             pltpu.VMEM((FEAT, D), F32),
             pltpu.VMEM((5, D, D), F32),
@@ -531,7 +610,7 @@
             pltpu.VMEM((5, G - 1, CH, D), F32),
             pltpu.VMEM((G - 1, EC, D), F32),
             column(),
-            dma((6,)),
+            dma((10,)), dma((6,)),
             dma((S, L)), dma((S, L)),
             dma((S * W,)), dma((S * W,)),
             dma((6, G - 1)), dma((6, G - 1)),
@@ -540,15 +619,19 @@
         compiler_params=pltpu.CompilerParams(
             collective_id=0, has_side_effects=True, vmem_limit_bytes=56 * 1024 * 1024
         ),
-    )(walkers, nuclei, w_embed, w_query, w_key, w_value, w_attn_out, w_mlp, b_mlp, w_out)
-    margins, g_query, g_key, g_value, g_attn, g_mlp, extra = outs
-    return (
-        margins,
-        extra[:, :FEAT],
-        g_query, g_key, g_value, g_attn, g_mlp,
-        extra[:, FEAT : FEAT + 1],
-        extra[:, FEAT + 1],
-    )
+    )(walkers, nuclei.T, w_embed, w_query, w_key, w_value, w_attn_out, w_mlp, b_mlp, w_out)
+    like = lambda x: jax.ShapeDtypeStruct(x.shape, F32)
+    return pl.pallas_call(
+        finish_kernel,
+        out_shape=(
+            jax.ShapeDtypeStruct((N, N), F32),
+            like(w_embed), weight, weight, weight, weight, weight, like(b_mlp), like(w_out),
+        ),
+        in_specs=[vmem] + [hbm] * 5 + [vmem],
+        out_specs=(vmem, vmem) + (hbm,) * 5 + (vmem, vmem),
+        scratch_shapes=[dma((5 * L,))],
+        compiler_params=pltpu.CompilerParams(vmem_limit_bytes=56 * 1024 * 1024),
+    )(*outs)
 
 
 def solution(mesh):

time: 102 us -> 175 us (1.72)
  Pallas kernels: 88.5 us -> 174 us
  local copies, waits for them, and re-layouts: 12 us -> 0 us
    pallas_call x0 -> x1, Pallas kernels: none -> 82.2 us  [shards(): pl.pallas_call(finish_kernel, out_shape=(jax.ShapeDtypeStruct((N, N), F32...]
    unnamed x18 -> x0, local copies, waits for them, and re-layouts: 9.05 us -> none
    pallas_call x1, Pallas kernels: 88.5 us -> 92.2 us  [shards(): pl.pallas_call(functools.partial(kernel, cfg), out_shape=(jax.ShapeDtypeS...]
    slice x2 -> x0, local copies, waits for them, and re-layouts: 2.91 us -> none  [the longest x1 1.54 us: shards(): extra[:, :FEAT]]
where the time goes in v1:
time: 175 us
  Pallas kernels  174 us (99%)
    pallas_call x1, Pallas kernels, shards(): pl.pallas_call(functools.partial(kernel, cfg), out_shape=(jax.ShapeDtypeS...  92.2 us
    pallas_call x1, Pallas kernels, shards(): pl.pallas_call(finish_kernel, out_shape=(jax.ShapeDtypeStruct((N, N), F32...  82.2 us

profile of v1, /device:TPU:0, one launch (start us, length us, event | category | flops | bytes accessed | tf_op | source)
XLA Modules:
  0.0 175.0 jit_solution(2988008527648583378)
XLA Ops:
  0.6 92.2 %shard_map.169 = (f32[8,8]{1,0:T(8,128)}, f32[2,1,256,256]{3,2,1,0:T(8,128)}, f32[2,1,256,256]{3,2,1,0:T(8,128)}, f32[2,1,256,256]{3,2,1,0:T(8,128)}, f32[2,1,25...) custom-call(f32[2,1,126]{2,1,0:T(1,128)} %walkers.1, f32[3,12]{1,0:T(4,128)} %bitcast.1, ...), custom_call_target="tpu_custom_call" | custom-call | tf_op jit(solution)/shard_map/pallas_call | solution.py:580
  92.9 82.2 %shard_map.170 = (f32[8,8]{1,0:T(8,128)}, f32[2,48,256]{2,1,0:T(8,128)}, f32[2,1,256,256]{3,2,1,0:T(8,128)}, f32[2,1,256,256]{3,2,1,0:T(8,128)}, f32[2,1,256,256...) custom-call(f32[8,8]{1,0:T(8,128)} %get-tuple-element.16.m_in, ...), custom_call_target="tpu_custom_call" | custom-call | tf_op jit(solution)/shard_map/pallas_call | solution.py:624

commit v2 on v1

--- a/solution.py
+++ b/solution.py
@@ -13,7 +13,7 @@
 F32 = jnp.float32
 BF16 = jnp.bfloat16
 MESH = pl.DeviceIdType.MESH
-WALKERS_PER_BLOCK = 4
+WALKERS_PER_BLOCK = 8
 
 NN = (((1,), (0,)), ((), ()))
 NT = (((1,), (1,)), ((), ()))
@@ -30,25 +30,31 @@
     return out
 
 
-def product(a, b, dims, parts):
-    total = None
-    for order in range(parts - 1, -1, -1):
-        for i in range(order + 1):
-            term = lax.dot_general(a[i], b[order - i], dims, preferred_element_type=F32)
-            total = term if total is None else total + term
-    return total
-
-
-def product_packed(a, b):
-    parts, width = len(a), b[0].shape[0]
-    stack = jnp.concatenate(b, axis=0)
+def terms(parts):
+    return [(i, order - i) for order in range(parts - 1, -1, -1) for i in range(order + 1)]
+
+
+def left(x, parts):
+    pieces = split(x, parts)
+    return jnp.concatenate([pieces[i] for i, _ in terms(parts)], axis=1)
+
+
+def right(x, parts):
+    pieces = split(x, parts)
+    return jnp.concatenate([pieces[i] for _, i in terms(parts)], axis=0)
+
+
+def matmul(a, b, dims=NN):
+    return lax.dot_general(a, b, dims, preferred_element_type=F32)
+
+
+def product(a, b, dims):
+    parts, rows = len(a), a[0].shape[0]
     sums = [None] * parts
-    for i in range(parts - 1, -1, -1):
-        wide = lax.dot_general(
-            a[i], stack[: (parts - i) * width], NT, preferred_element_type=F32
-        )
-        for n in range(parts - i):
-            term = wide[:, n * width : (n + 1) * width]
+    for n in range(parts - 1, -1, -1):
+        tall = matmul(jnp.concatenate(a[: parts - n], axis=0), b[n], dims)
+        for i in range(parts - n):
+            term = tall[i * rows : (i + 1) * rows]
             sums[i + n] = term if sums[i + n] is None else sums[i + n] + term
     total = sums[-1]
     for term in sums[-2::-1]:
@@ -73,7 +79,7 @@
     cfg,
     walkers, nuclei_in, w_embed, w_query, w_key, w_value, w_attn, w_mlp, b_mlp_in, w_out_in,
     margins, f_mlp, f_attn, f_value, f_key, f_query, f_extra,
-    o_weights, o_extra, nuclei, b_mlp, w_out, wbuf, raw_embed, raw, vecs, s_embed, s_w, feats, x1, r1, q, k, v, att, mixed, x2, r2, act, h2,
+    o_weights, o_extra, nuclei, b_mlp, w_out, wbuf, raw_embed, raw, vecs, s_embed, s_qk, s_w, s_qkvt, s_t, spots, feats, x1, r1, q, k, v, att, mixed, x2, r2, act, h2,
     g1, gk, gq, gv, dm, lrow, tab, part, part_extra, rbuf, rbuf_extra, ccol,
     load_sem, flush_sem, walk_send, walk_recv, tab_send, tab_recv, rs_send, rs_recv, ag_send, ag_recv,
 ):
@@ -91,7 +97,7 @@
     net = s * L + j
     me = s * W + w
 
-    loads = [pltpu.make_async_copy(w_embed.at[j], raw_embed, load_sem.at[0])]
+    loads = [pltpu.make_async_copy(w_embed.at[j], raw_embed.at[pl.ds(0, FEAT)], load_sem.at[0])]
     for n, ref in enumerate((w_query, w_key, w_value, w_attn, w_mlp)):
         loads.append(pltpu.make_async_copy(ref.at[j, 0], raw.at[n], load_sem.at[1 + n]))
     for n, (src, dst) in enumerate(((nuclei_in, nuclei), (b_mlp_in, b_mlp), (w_out_in, w_out))):
@@ -110,13 +116,16 @@
 
     lax.fori_loop(1, S * W, greet, 0)
 
+    raw_embed[FEAT:, :] = jnp.zeros((128 - FEAT, D), F32)
     for copy in loads:
         copy.wait()
-    for i, piece in enumerate(split(raw_embed[...], 3)):
-        s_embed[i] = piece
-    for n in range(5):
-        for i, piece in enumerate(split(raw[n], 3 if n < 2 else 2)):
-            s_w[n, i] = piece
+    s_embed[...] = right(raw_embed[...], 3)
+    s_qk[...] = jnp.concatenate([right(raw[0], 3), right(raw[1], 3)], axis=1)
+    for n in range(3):
+        s_w[n] = right(raw[2 + n], 2)
+        s_qkvt[n] = right(raw[n].T, 2)
+    for n in range(2):
+        s_t[n] = right(raw[3 + n].T, 2)
     vecs[0:1, :] = b_mlp[j]
     vecs[1:2, :] = w_out[pl.ds(j, 1), :]
 
@@ -165,9 +174,15 @@
             along = jnp.where(atom == a, nuclei[c : c + 1, a : a + 1], along)
         nuc.append(along)
     kind = lax.rem(lane, 4)
-    row_of = lax.broadcasted_iota(jnp.int32, (PAD, 3 * NE), 0)
-    col_of = lax.broadcasted_iota(jnp.int32, (PAD, 3 * NE), 1)
-    pick = [col_of == row_of * 3 + c for c in range(3)]
+    mine_of = (
+        lax.div(lax.broadcasted_iota(jnp.int32, (PAD, 3 * NE), 1), 3)
+        == lax.broadcasted_iota(jnp.int32, (PAD, 3 * NE), 0)
+    )
+    spread = (
+        lax.rem(lax.broadcasted_iota(jnp.int32, (3 * NE, 384), 0), 3)
+        == lax.div(lax.broadcasted_iota(jnp.int32, (3 * NE, 384), 1), 128)
+    )
+    spread = jnp.where(spread, 1.0, 0.0).astype(BF16)
     live = lax.broadcasted_iota(jnp.int32, (PAD, 1), 0) < NE
 
     for s_from in range(S):
@@ -189,21 +204,22 @@
     for i in range(N):
         for x in range(L):
             row = wbuf[i // L, x, i % L]
-            pos = [
-                jnp.sum(jnp.where(pick[c], row, 0.0), axis=1, keepdims=True) for c in range(3)
-            ]
-            off = [pos[c] - nuc[c] for c in range(3)]
-            dist = jnp.sqrt(off[0] * off[0] + off[1] * off[1] + off[2] * off[2] + 1.0)
-            f = jnp.where(
-                kind == 0, off[0], jnp.where(kind == 1, off[1], jnp.where(kind == 2, off[2], dist))
-            )
             p = i * L + x
-            feats[p * PAD : (p + 1) * PAD, :] = f[:, :FEAT]
+            spots[p * PAD : (p + 1) * PAD, :] = jnp.where(mine_of, row, 0.0)
+
+    def features(rows):
+        parts = split(spots[rows, :], 3)
+        pos = matmul(parts[2], spread) + matmul(parts[1], spread) + matmul(parts[0], spread)
+        off = [pos[:, c * 128 : (c + 1) * 128] - nuc[c] for c in range(3)]
+        dist = jnp.sqrt(off[0] * off[0] + off[1] * off[1] + off[2] * off[2] + 1.0)
+        f = jnp.where(
+            kind == 0, off[0], jnp.where(kind == 1, off[1], jnp.where(kind == 2, off[2], dist))
+        )
+        return jnp.where(lane < FEAT, f, 0.0)
 
     head_of = lax.div(lax.broadcasted_iota(jnp.int32, (1, D), 1), head_size)
     head_mask = [jnp.where(head_of == h, 1.0, 0.0).astype(F32) for h in range(HEADS)]
     head_mask_bf16 = [mask.astype(BF16) for mask in head_mask]
-    key_live = lax.broadcasted_iota(jnp.int32, (1, PAD), 1) < NE
 
     def stack_heads(x):
         return jnp.concatenate([x * head_mask_bf16[h] for h in range(HEADS)], axis=0)
@@ -213,44 +229,41 @@
 
     lrow[...] = jnp.zeros_like(lrow)
 
-    def weights(n, parts):
-        return [s_w[n, i] for i in range(parts)]
-
     def forward(b, carry):
         rows = pl.ds(pl.multiple_of(b * RB, RB), RB)
-        h0 = product(split(feats[rows, :], 3), [s_embed[i] for i in range(3)], NN, 3)
+        f = features(rows)
+        feats[rows, :] = f
+        h0 = matmul(left(f, 3), s_embed[...])
         normed, scale = normalise(h0)
         x1[rows, :] = normed
         r1[rows, :] = scale
-        xs = split(normed, 3)
-        queries = product(xs, weights(0, 3), NN, 3)
-        keys = product(xs, weights(1, 3), NN, 3)
-        values = product(xs[:2], weights(2, 2), NN, 2)
+        both = matmul(left(normed, 3), s_qk[...])
+        queries, keys = both[:, :D], both[:, D:]
+        values = matmul(left(normed, 2), s_w[0])
         q[rows, :] = queries
         k[rows, :] = keys
         v[rows, :] = values
-        queries_split = split(queries, 3)
+        qs = split(queries, 3)
         ks = split(keys, 3)
         vs = split(values, 2)
         outs = []
         for i in range(WB):
             here = slice(i * PAD, (i + 1) * PAD)
-            qs = [stack_heads(piece[here]) for piece in queries_split]
-            scores = product_packed(qs, [piece[here] for piece in ks]) / math.sqrt(head_size)
-            scores = jnp.where(key_live, scores, -1e30)
-            e = jnp.exp(scores - jnp.max(scores, axis=-1, keepdims=True))
-            a = e / jnp.sum(e, axis=-1, keepdims=True)
+            scores = product(
+                [piece[here] for piece in ks], [stack_heads(piece[here]) for piece in qs], NT
+            ) / math.sqrt(head_size)
+            scores = jnp.where(live, scores, -1e30)
+            e = jnp.exp(scores - jnp.max(scores, axis=0, keepdims=True))
+            a = e / jnp.sum(e, axis=0, keepdims=True)
             att[b * WB + i] = a
-            outs.append(
-                merge_heads(product(split(a, 2), [piece[here] for piece in vs], NN, 2))
-            )
+            outs.append(merge_heads(product(split(a.T, 2), [piece[here] for piece in vs], NN)))
         mix = jnp.concatenate(outs, axis=0)
         mixed[rows, :] = mix
-        h1 = h0 + product(split(mix, 2), weights(3, 2), NN, 2)
+        h1 = h0 + matmul(left(mix, 2), s_w[1])
         normed2, scale2 = normalise(h1)
         x2[rows, :] = normed2
         r2[rows, :] = scale2
-        t = jnp.tanh(product(split(normed2, 2), weights(4, 2), NN, 2) + vecs[0:1, :])
+        t = jnp.tanh(matmul(left(normed2, 2), s_w[2]) + vecs[0:1, :])
         act[rows, :] = t
         last = h1 + t
         h2[rows, :] = last
@@ -287,11 +300,11 @@
         gh = vecs[1:2, :] * (1.0 / NE)
         t = act[rows, :]
         dinner = gh * (1.0 - t * t)
-        dx2 = product(split(dinner, 2), weights(4, 2), NT, 2)
+        dx2 = matmul(left(dinner, 2), s_t[1])
         act[rows, :] = dinner
         dh1 = gh + normalise_back(dx2, x2[rows, :], r2[rows, :])
         g1[rows, :] = dh1
-        dm[rows, :] = product(split(dh1, 2), weights(3, 2), NT, 2)
+        dm[rows, :] = matmul(left(dh1, 2), s_t[0])
         return carry
 
     lax.fori_loop(0, blocks, backward_top, 0)
@@ -458,7 +471,7 @@
     c = ccol[...]
 
     def outer(x, y):
-        return product(split(x, 2), split(y * c, 2), TN, 2)
+        return matmul(left(x.T, 2), right(y * c, 2))
 
     part[0] = outer(x2[...], act[...])
     rs_start(0)
@@ -471,7 +484,7 @@
     def backward_values(b, carry):
         for i in range(WB):
             here = pl.ds(pl.multiple_of(b * RB + i * PAD, PAD), PAD)
-            gv[here, :] = product(split(att[b * WB + i], 2), stacked_gradient(here), TN, 2)
+            gv[here, :] = product(split(att[b * WB + i], 2), stacked_gradient(here), NN)
         return carry
 
     lax.fori_loop(0, blocks, backward_values, 0)
@@ -486,11 +499,10 @@
             a = att[b * WB + i]
             ks = split(k[here, :], 2)
             qs = [stack_heads(p) for p in split(q[here, :], 2)]
-            da = product_packed(stacked_gradient(here), split(v[here, :], 2))
-            ds = a * (da - jnp.sum(a * da, axis=-1, keepdims=True)) / math.sqrt(head_size)
-            dss = split(ds, 2)
-            gq[here, :] = merge_heads(product(dss, ks, NN, 2))
-            gk[here, :] = product(dss, qs, TN, 2)
+            da = product(split(v[here, :], 2), stacked_gradient(here), NT)
+            ds = a * (da - jnp.sum(a * da, axis=0, keepdims=True)) / math.sqrt(head_size)
+            gq[here, :] = merge_heads(product(split(ds.T, 2), ks, NN))
+            gk[here, :] = product(split(ds, 2), qs, NN)
 
         for bb in range(blocks):
             arrays = ((0, 2), (0, 1), (0, 1, 2), (0, 1, 2))[bb % 4] if bb < 4 else ()
@@ -503,18 +515,19 @@
 
     lax.fori_loop(0, blocks, backward_scores, 0)
 
-    part[3] = outer(x1[...], gk[...])
+    x1_left = left(x1[...].T, 2)
+    part[3] = matmul(x1_left, right(gk[...] * c, 2))
     rs_start(3)
-    part[4] = outer(x1[...], gq[...])
+    part[4] = matmul(x1_left, right(gq[...] * c, 2))
     rs_start(4)
     advance(1, 2)
 
     def backward_embed(b, carry):
         rows = pl.ds(pl.multiple_of(b * RB, RB), RB)
         dx1 = (
-            product(split(gq[rows, :], 2), weights(0, 2), NT, 2)
-            + product(split(gk[rows, :], 2), weights(1, 2), NT, 2)
-            + product(split(gv[rows, :], 2), weights(2, 2), NT, 2)
+            matmul(left(gq[rows, :], 2), s_qkvt[0])
+            + matmul(left(gk[rows, :], 2), s_qkvt[1])
+            + matmul(left(gv[rows, :], 2), s_qkvt[2])
         )
         dm[rows, :] = g1[rows, :] + normalise_back(dx1, x1[rows, :], r1[rows, :])
         return carry
@@ -522,7 +535,7 @@
     lax.fori_loop(0, blocks, backward_embed, 0)
     advance(3, 4, 2)
     part_extra[...] = jnp.zeros_like(part_extra)
-    part_extra[0:FEAT, :] = outer(feats[...], dm[...])
+    part_extra[0:FEAT, :] = outer(feats[...], dm[...])[:FEAT]
     part_extra[FEAT : FEAT + 1, :] = jnp.sum(act[...] * c, axis=0, keepdims=True)
     part_extra[FEAT + 1 : FEAT + 2, :] = jnp.sum(h2[...] * c, axis=0, keepdims=True) / NE
     rs_start(5)
@@ -537,16 +550,20 @@
 
 def finish_kernel(
     m_in, mlp, attn, value, key, query, extra,
-    margins, o_embed, o_query, o_key, o_value, o_attn, o_mlp, o_bias, o_out, sem,
+    margins, o_embed, o_query, o_key, o_value, o_attn, o_mlp, o_bias, o_out, held, sem,
 ):
     feat = o_embed.shape[1]
     margins[...] = m_in[...]
-    copies = []
-    for src, dst in ((query, o_query), (key, o_key), (value, o_value), (attn, o_attn), (mlp, o_mlp)):
-        for n in range(dst.shape[0]):
-            copies.append(pltpu.make_async_copy(src.at[n], dst.at[n], sem.at[len(copies)]))
-    for copy in copies:
+    pairs = ((query, o_query), (key, o_key), (value, o_value), (attn, o_attn), (mlp, o_mlp))
+    ins = [pltpu.make_async_copy(src, held.at[n], sem.at[n]) for n, (src, _) in enumerate(pairs)]
+    copies = [
+        pltpu.make_async_copy(held.at[n], dst, sem.at[5 + n]) for n, (_, dst) in enumerate(pairs)
+    ]
+    for copy in ins:
         copy.start()
+    for n in range(5):
+        ins[n].wait()
+        copies[n].start()
     for n in range(o_embed.shape[0]):
         o_embed[n] = extra[n, :feat]
         o_bias[n] = extra[n, feat : feat + 1]
@@ -593,14 +610,18 @@
             pltpu.VMEM(b_mlp.shape, F32),
             pltpu.VMEM(w_out.shape, F32),
             pltpu.VMEM((S, L, L, 1, coords), F32),
-            pltpu.VMEM((FEAT, D), F32),
+            pltpu.VMEM((128, D), F32),
             pltpu.VMEM((5, D, D), F32),
             pltpu.VMEM((8, D), F32),
-            pltpu.VMEM((3, FEAT, D), BF16),
-            pltpu.VMEM((5, 3, D, D), BF16),
-            pltpu.VMEM((R, FEAT), F32),
+            pltpu.VMEM((6 * 128, D), BF16),
+            pltpu.VMEM((6 * D, 2 * D), BF16),
+            pltpu.VMEM((3, 3 * D, D), BF16),
+            pltpu.VMEM((3, 3 * D, D), BF16),
+            pltpu.VMEM((2, 3 * D, D), BF16),
+            pltpu.VMEM((R, coords), F32),
+            pltpu.VMEM((R, 128), F32),
             full(), column(), full(), full(), full(),
-            pltpu.VMEM((held, HEADS * PAD, PAD), F32),
+            pltpu.VMEM((held, PAD, HEADS * PAD), F32),
             full(), full(), column(), full(), full(),
             full(), full(), full(), full(), full(),
             pltpu.VMEM((1, 128), F32),
@@ -629,7 +650,7 @@
         ),
         in_specs=[vmem] + [hbm] * 5 + [vmem],
         out_specs=(vmem, vmem) + (hbm,) * 5 + (vmem, vmem),
-        scratch_shapes=[dma((5 * L,))],
+        scratch_shapes=[pltpu.VMEM((5, L, 1, D, D), F32), dma((10,))],
         compiler_params=pltpu.CompilerParams(vmem_limit_bytes=56 * 1024 * 1024),
     )(*outs)
 

time: 175 us -> 85.9 us (0.49)
  Pallas kernels: 174 us -> 85 us
    pallas_call x1, Pallas kernels: 82.2 us -> 4.17 us  [shards(): pl.pallas_call(finish_kernel, out_shape=(jax.ShapeDtypeStruct((N, N), F32...]
    pallas_call x1, Pallas kernels: 92.2 us -> 80.8 us  [shards(): pl.pallas_call(functools.partial(kernel, cfg), out_shape=(jax.ShapeDtypeS...]
where the time goes in v2:
time: 85.9 us; the launch traced here: 85.7 us
  Pallas kernels  85 us (99%)
    pallas_call x1, Pallas kernels, shards(): pl.pallas_call(functools.partial(kernel, cfg), out_shape=(jax.ShapeDtypeS...  80.8 us
    pallas_call x1, Pallas kernels, shards(): pl.pallas_call(finish_kernel, out_shape=(jax.ShapeDtypeStruct((N, N), F32...  4.17 us

profile of v2, /device:TPU:0, one launch (start us, length us, event | category | flops | bytes accessed | tf_op | source)
XLA Modules:
  0.0 85.7 jit_solution(6210189708022633573)
XLA Ops:
  0.6 80.8 %shard_map.169 = (f32[8,8]{1,0:T(8,128)}, f32[2,1,256,256]{3,2,1,0:T(8,128)}, f32[2,1,256,256]{3,2,1,0:T(8,128)}, f32[2,1,256,256]{3,2,1,0:T(8,128)}, f32[2,1,25...) custom-call(f32[2,1,126]{2,1,0:T(1,128)} %walkers.1, f32[3,12]{1,0:T(4,128)} %bitcast.1, ...), custom_call_target="tpu_custom_call" | custom-call | tf_op jit(solution)/shard_map/pallas_call | solution.py:597
  81.5 4.2 %shard_map.170 = (f32[8,8]{1,0:T(8,128)}, f32[2,48,256]{2,1,0:T(8,128)}, f32[2,1,256,256]{3,2,1,0:T(8,128)}, f32[2,1,256,256]{3,2,1,0:T(8,128)}, f32[2,1,256,256...) custom-call(f32[8,8]{1,0:T(8,128)} %get-tuple-element.16.m_in, ...), custom_call_target="tpu_custom_call" | custom-call | tf_op jit(solution)/shard_map/pallas_call | solution.py:645

commit v3 on v2

--- a/solution.py
+++ b/solution.py
@@ -361,26 +361,55 @@
     outs = [o_weights.at[m] for m in range(5)] + [o_extra]
     results = (f_mlp, f_attn, f_value, f_key, f_query, f_extra)
 
-    def rs_copy(m, d):
-        to = lax.rem(g + d, G)
+    bits = G.bit_length() - 1
+    own_bit = [lax.rem(lax.div(g, 1 << i), 2) for i in range(bits)]
+
+    def rs_rows(m, block):
         if m < 5:
-            src = part.at[m, pl.ds(pl.multiple_of(to * CH, CH), CH)]
-            dst = rbuf.at[m, d - 1]
-        else:
-            src = part_extra.at[pl.ds(pl.multiple_of(to * EC, EC), EC)]
-            dst = rbuf_extra.at[d - 1]
-        return pltpu.make_async_remote_copy(
-            src_ref=src,
-            dst_ref=dst,
-            send_sem=rs_send.at[m, d - 1],
-            recv_sem=rs_recv.at[m, d - 1],
-            device_id=(s, j * G + to),
-            device_id_type=MESH,
-        )
-
-    def rs_start(m):
-        for d in range(1, G):
-            rs_copy(m, d).start()
+            return part.at[m, pl.ds(pl.multiple_of(block * CH, CH), CH)]
+        return part_extra.at[pl.ds(pl.multiple_of(block * EC, EC), EC)]
+
+    def rs_slot(m, n):
+        return rbuf.at[m, n] if m < 5 else rbuf_extra.at[n]
+
+    def rs_stage(m, stage):
+        order = range(bits) if m % 2 else range(bits - 1, -1, -1)
+        order = list(order)
+        bit, rest = order[stage], order[stage + 1 :]
+        fixed = sum((own_bit[i] * (1 << i) for i in order[:stage]), 0)
+        first = sum(G >> (i + 1) for i in range(stage))
+        partner = g + (1 - 2 * own_bit[bit]) * (1 << bit)
+        copies, kept = [], []
+        for n in range(1 << len(rest)):
+            free = sum(((n >> i) & 1) << place for i, place in enumerate(rest))
+            sent = fixed + (1 - own_bit[bit]) * (1 << bit) + free
+            kept.append((first + n, fixed + own_bit[bit] * (1 << bit) + free))
+            copies.append(
+                pltpu.make_async_remote_copy(
+                    src_ref=rs_rows(m, sent),
+                    dst_ref=rs_slot(m, first + n),
+                    send_sem=rs_send.at[m, first + n],
+                    recv_sem=rs_recv.at[m, first + n],
+                    device_id=(s, j * G + partner),
+                    device_id_type=MESH,
+                )
+            )
+        return copies, kept
+
+    def rs_start(m, stage=0):
+        for copy in rs_stage(m, stage)[0]:
+            copy.start()
+
+    def rs_add(m, stage):
+        copies, kept = rs_stage(m, stage)
+        for copy, (n, block) in zip(copies, kept):
+            copy.wait_recv()
+            rows = rs_rows(m, block)
+            rows[...] = rows[...] + rs_slot(m, n)[...]
+
+    def rs_finish(m):
+        rs_add(m, bits - 1)
+        piece(m, w)[...] = rs_rows(m, g)[...]
 
     def piece(m, who):
         jj = lax.div(who, G)
@@ -388,20 +417,6 @@
         if m < 5:
             return outs[m].at[jj, 0, pl.ds(pl.multiple_of(gg * CH, CH), CH)]
         return outs[m].at[jj, pl.ds(pl.multiple_of(gg * EC, EC), EC)]
-
-    def rs_finish(m):
-        for d in range(1, G):
-            rs_copy(m, d).wait_recv()
-        if m < 5:
-            total = part[m, pl.ds(pl.multiple_of(g * CH, CH), CH)]
-            for d in range(1, G):
-                total = total + rbuf[m, d - 1]
-            outs[m][j, 0, pl.ds(pl.multiple_of(g * CH, CH), CH)] = total
-        else:
-            total = part_extra[pl.ds(pl.multiple_of(g * EC, EC), EC)]
-            for d in range(1, G):
-                total = total + rbuf_extra[d - 1]
-            outs[m][j, pl.ds(pl.multiple_of(g * EC, EC), EC)] = total
 
     odd = lax.rem(w, 2)
     place = (1 - odd) * lax.div(w, 2) + odd * (W - lax.div(w + 1, 2))
@@ -458,15 +473,31 @@
                 ag_copy(m, way, t).wait_send()
         flush(m).wait()
 
-    todo = [[("sum", 0)] + [("hop", t) for t in range(1, last + 1)] for m in range(6)]
+    todo = [[("half", n) for n in range(bits - 1)] + [("sum", 0)] + [("hop", t) for t in range(1, last + 1)] for m in range(6)]
+
+    def take(*arrays):
+        return [(m,) + todo[m].pop(0) for m in arrays if todo[m]]
+
+    def act_on(steps):
+        for m, what, t in steps:
+            if what == "half":
+                rs_add(m, t)
+                rs_start(m, t + 1)
+                continue
+            if what == "sum":
+                rs_finish(m)
+            ag_step(m, t)
 
     def advance(*arrays):
-        for m in arrays:
-            if todo[m]:
-                what, t = todo[m].pop(0)
-                if what == "sum":
-                    rs_finish(m)
-                ag_step(m, t)
+        act_on(take(*arrays))
+
+    def at(plan, b, i):
+        for (block, place), steps in plan.items():
+            if place == i:
+
+                @pl.when(b == block)
+                def _():
+                    act_on(steps)
 
     c = ccol[...]
 
@@ -485,13 +516,14 @@
         for i in range(WB):
             here = pl.ds(pl.multiple_of(b * RB + i * PAD, PAD), PAD)
             gv[here, :] = product(split(att[b * WB + i], 2), stacked_gradient(here), NN)
+        at(value_plan, b, 0)
         return carry
 
+    value_plan = {(0, 0): take(0), (1, 0): take(0, 1)}
     lax.fori_loop(0, blocks, backward_values, 0)
     part[2] = outer(x1[...], gv[...])
     rs_start(2)
-    advance(0)
-    advance(1)
+    advance(0, 1)
 
     def backward_scores(b, carry):
         for i in range(WB):
@@ -503,24 +535,23 @@
             ds = a * (da - jnp.sum(a * da, axis=0, keepdims=True)) / math.sqrt(head_size)
             gq[here, :] = merge_heads(product(split(ds.T, 2), ks, NN))
             gk[here, :] = product(split(ds, 2), qs, NN)
-
-        for bb in range(blocks):
-            arrays = ((0, 2), (0, 1), (0, 1, 2), (0, 1, 2))[bb % 4] if bb < 4 else ()
-
-            @pl.when(b == bb)
-            def _():
-                advance(*arrays)
+            at(score_plan, b, i)
 
         return carry
 
+    score_plan = {
+        (0, 1): take(0), (0, 3): take(1, 2), (0, 5): take(0, 2), (0, 7): take(1),
+        (1, 1): take(0, 2), (1, 3): take(1, 2), (1, 5): take(1), (1, 7): take(2),
+    }
     lax.fori_loop(0, blocks, backward_scores, 0)
 
     x1_left = left(x1[...].T, 2)
     part[3] = matmul(x1_left, right(gk[...] * c, 2))
     rs_start(3)
+    advance(2)
     part[4] = matmul(x1_left, right(gq[...] * c, 2))
     rs_start(4)
-    advance(1, 2)
+    advance(3)
 
     def backward_embed(b, carry):
         rows = pl.ds(pl.multiple_of(b * RB, RB), RB)
@@ -530,10 +561,11 @@
             + matmul(left(gv[rows, :], 2), s_qkvt[2])
         )
         dm[rows, :] = g1[rows, :] + normalise_back(dx1, x1[rows, :], r1[rows, :])
+        at(embed_plan, b, 0)
         return carry
 
+    embed_plan = {(0, 0): take(3, 4), (1, 0): take(3, 4)}
     lax.fori_loop(0, blocks, backward_embed, 0)
-    advance(3, 4, 2)
     part_extra[...] = jnp.zeros_like(part_extra)
     part_extra[0:FEAT, :] = outer(feats[...], dm[...])[:FEAT]
     part_extra[FEAT : FEAT + 1, :] = jnp.sum(act[...] * c, axis=0, keepdims=True)
@@ -544,8 +576,9 @@
         advance(*range(6))
     for m in range(6):
         ag_finish(m)
-        for d in range(1, G):
-            rs_copy(m, d).wait_send()
+        for stage in range(bits):
+            for copy in rs_stage(m, stage)[0]:
+                copy.wait_send()
 
 
 def finish_kernel(
@@ -555,13 +588,17 @@
     feat = o_embed.shape[1]
     margins[...] = m_in[...]
     pairs = ((query, o_query), (key, o_key), (value, o_value), (attn, o_attn), (mlp, o_mlp))
-    ins = [pltpu.make_async_copy(src, held.at[n], sem.at[n]) for n, (src, _) in enumerate(pairs)]
+    L = o_embed.shape[0]
+    places = [(n, i) for n in range(5) for i in range(L)]
+    ins = [
+        pltpu.make_async_copy(pairs[n][0].at[i], held.at[n, i], sem.at[0, n, i]) for n, i in places
+    ]
     copies = [
-        pltpu.make_async_copy(held.at[n], dst, sem.at[5 + n]) for n, (_, dst) in enumerate(pairs)
+        pltpu.make_async_copy(held.at[n, i], pairs[n][1].at[i], sem.at[1, n, i]) for n, i in places
     ]
     for copy in ins:
         copy.start()
-    for n in range(5):
+    for n in range(len(places)):
         ins[n].wait()
         copies[n].start()
     for n in range(o_embed.shape[0]):
@@ -650,7 +687,7 @@
         ),
         in_specs=[vmem] + [hbm] * 5 + [vmem],
         out_specs=(vmem, vmem) + (hbm,) * 5 + (vmem, vmem),
-        scratch_shapes=[pltpu.VMEM((5, L, 1, D, D), F32), dma((10,))],
+        scratch_shapes=[pltpu.VMEM((5, L, 1, D, D), F32), dma((2, 5, L))],
         compiler_params=pltpu.CompilerParams(vmem_limit_bytes=56 * 1024 * 1024),
     )(*outs)
 

time: 85.9 us -> 105 us (1.22)
  Pallas kernels: 85 us -> 105 us
    pallas_call x1, Pallas kernels: 80.8 us -> 100 us  [shards(): pl.pallas_call(functools.partial(kernel, cfg), out_shape=(jax.ShapeDtypeS...]
where the time goes in v3:
time: 105 us
  Pallas kernels  105 us (100%)
    pallas_call x1, Pallas kernels, shards(): pl.pallas_call(functools.partial(kernel, cfg), out_shape=(jax.ShapeDtypeS...  100 us
    pallas_call x1, Pallas kernels, shards(): pl.pallas_call(finish_kernel, out_shape=(jax.ShapeDtypeStruct((N, N), F32...  4.16 us

profile of v3, /device:TPU:0, one launch (start us, length us, event | category | flops | bytes accessed | tf_op | source)
XLA Modules:
  0.0 105.2 jit_solution(357553743322885376)
XLA Ops:
  0.6 100.3 %shard_map.169 = (f32[8,8]{1,0:T(8,128)}, f32[2,1,256,256]{3,2,1,0:T(8,128)}, f32[2,1,256,256]{3,2,1,0:T(8,128)}, f32[2,1,256,256]{3,2,1,0:T(8,128)}, f32[2,1,25...) custom-call(f32[2,1,126]{2,1,0:T(1,128)} %walkers.1, f32[3,12]{1,0:T(4,128)} %bitcast.1, ...), custom_call_target="tpu_custom_call" | custom-call | tf_op jit(solution)/shard_map/pallas_call | solution.py:634
  101.0 4.2 %shard_map.170 = (f32[8,8]{1,0:T(8,128)}, f32[2,48,256]{2,1,0:T(8,128)}, f32[2,1,256,256]{3,2,1,0:T(8,128)}, f32[2,1,256,256]{3,2,1,0:T(8,128)}, f32[2,1,256,256...) custom-call(f32[8,8]{1,0:T(8,128)} %get-tuple-element.16.m_in, ...), custom_call_target="tpu_custom_call" | custom-call | tf_op jit(solution)/shard_map/pallas_call | solution.py:682
